TPU v7x, 32 devices: a whole 2x2x4 slice. The times are simulated.
32 devices in a mesh: scen: 4 (over y, x), gx: 2 (over core), gy: 4 (over z).
Axes of the slice: x: 2, y: 2, z: 4, core: 2. Of those that a mesh axis runs over, the one named last changes fastest.
Arguments:
- perm_log: float32 [2, 128, 512], P(None, 'gx', 'gy'), may hold values from -2.5 to 2.5
- facies: int32 [2, 128, 512], P(None, 'gx', 'gy'), may hold values from 0 to 3
- facies_scale: float32 [4], replicated, may hold values from 0.5 to 2
- accumulation: float32 [2, 128, 512], P(None, 'gx', 'gy'), may hold values from 0.05 to 0.5
- previous_pressure: float32 [4, 2, 128, 512], P('scen', None, 'gx', 'gy'), may hold values from -6 to 6
- observed: float32 [4, 2, 128, 512], P('scen', None, 'gx', 'gy'), may hold values from -6 to 6
- well_cells: int32 [4, 5], P('scen'), may hold values from 0 to 131071
- well_rates: float32 [4, 5], P('scen'), may hold values from 5 to 20
Outputs:
- pressure: float32 [4, 2, 128, 512], P('scen', None, 'gx', 'gy')
- adjoint: float32 [4, 2, 128, 512], P('scen', None, 'gx', 'gy')
- gradient: float32 [2, 128, 512], P(None, 'gx', 'gy')
Inputs may be any that keep to these rules, and one draw needn't show every extreme that they name: `well_cells`: a flat index layer * 128 * 512 + row * 512 + column of a grid cell; several wells may share a cell.
All inputs are finite; a program needn't handle non-finite values.
Results may differ from a plain program's by a relative error of at most 0.0001.
Values sent between devices are 32-bit elements; how exact they have to be, the bound alone decides.
No kernel may reach another device: no remote copies, remote signals or barrier semaphores. Data moves between devices by JAX's collectives and lax.ppermute only.
A program may use at most 128 MiB of HBM per device.

v0:
```python
from functools import partial

import jax
import jax.numpy as jnp
from jax import lax
from jax.experimental import pallas as pl
from jax.experimental.pallas import tpu as pltpu
from jax.sharding import PartitionSpec as P

WELLS = 5
FACIES = 4
LAYERS = 2
SMOOTH = 2
COARSE = 4

vertical = 0.3
damping = 0.8

LANES = 128
HALF = 64
SUB = 8
PERM, ACC, PREV, OBS = range(4)


def lane_index():
    return lax.broadcasted_iota(jnp.int32, (SUB, LANES), 1)


def row_index():
    return lax.broadcasted_iota(jnp.int32, (SUB, LANES), 0)


def lane_roll(value, shift):
    return pltpu.roll(value, shift % LANES, value.ndim - 1)


def row_roll(value, shift):
    return pltpu.roll(value, shift % SUB, 0)


def pack_kernel(scale_hbm, perm_log_hbm, facies_hbm, acc_hbm, prev_hbm, obs_hbm, own, to_left, to_right,
                scale, perm_log, facies, acc, prev, obs, sems):
    pairs = ((scale_hbm, scale), (perm_log_hbm, perm_log), (facies_hbm, facies), (acc_hbm, acc), (prev_hbm, prev),
             (obs_hbm, obs))
    copies = [pltpu.make_async_copy(source, target, sems.at[i]) for i, (source, target) in enumerate(pairs)]
    for copy in copies:
        copy.start()
    for copy in copies:
        copy.wait()
    label = facies[...]
    factor = jnp.zeros(label.shape, jnp.float32)
    for number in range(FACIES):
        factor = factor + jnp.where(label == number, scale[number], jnp.float32(0.0))
    fields = (jnp.exp(perm_log[...]) * factor, acc[...], prev[0], obs[0])
    low = lax.broadcasted_iota(jnp.int32, label.shape, 2) < HALF
    for number in range(4):
        own[number] = fields[number]
    for pair in range(2):
        first, second = fields[2 * pair], lane_roll(fields[2 * pair + 1], HALF)
        to_left[pair] = jnp.where(low, first, second)
        to_right[pair] = jnp.where(low, second, first)


def merge_kernel(from_right, from_left, beside):
    low = lax.broadcasted_iota(jnp.int32, beside.shape[1:], 2) < HALF
    for pair in range(2):
        right, left = from_right[pair], from_left[pair]
        beside[2 * pair] = jnp.where(low, right, left)
        beside[2 * pair + 1] = lane_roll(jnp.where(low, left, right), HALF)


class Level:
    def __init__(self, count, span, refs):
        self.count = count
        self.span = span
        (self.c_north, self.c_south, self.c_west, self.c_east, self.c_layer, self.weight, self.diag, self.target,
         self.now, self.later) = refs

    def keys(self, blocks):
        for b in range(blocks):
            for t in range(self.count):
                for u in range(2):
                    for layer in range(LAYERS):
                        yield layer, u, b, t


def east_of(pair, span):
    edge = lane_index() >= LANES - span
    rolled = [lane_roll(value, -span) for value in pair]
    return [jnp.where(edge, rolled[1 - u], rolled[u]) for u in range(2)]


def west_of(pair, span):
    edge = lane_index() < span
    rolled = [lane_roll(value, span) for value in pair]
    return [jnp.where(edge, rolled[1 - u], rolled[u]) for u in range(2)]


def row_before(values, blocks):
    edge = row_index() < 1
    rolled = [row_roll(value, 1) for value in values]
    return [jnp.where(edge, rolled[(b - 1) % blocks], rolled[b]) for b in range(blocks)]


def row_after(values, blocks):
    edge = row_index() >= SUB - 1
    rolled = [row_roll(value, -1) for value in values]
    return [jnp.where(edge, rolled[(b + 1) % blocks], rolled[b]) for b in range(blocks)]


def neighbour_sums(level, source, blocks):
    last = level.count - 1
    before, after = {}, {}
    for layer in range(LAYERS):
        for u in range(2):
            lows = row_before([source[layer, u, b, last] for b in range(blocks)], blocks)
            highs = row_after([source[layer, u, b, 0] for b in range(blocks)], blocks)
            for b in range(blocks):
                before[layer, u, b] = lows[b]
                after[layer, u, b] = highs[b]
    for b in range(blocks):
        for t in range(level.count):
            here = [[source[layer, u, b, t] for u in range(2)] for layer in range(LAYERS)]
            for layer in range(LAYERS):
                east = east_of(here[layer], level.span)
                west = west_of(here[layer], level.span)
                for u in range(2):
                    north = source[layer, u, b, t - 1] if t > 0 else before[layer, u, b]
                    south = source[layer, u, b, t + 1] if t < last else after[layer, u, b]
                    key = layer, u, b, t
                    total = (level.c_north[key] * north + level.c_south[key] * south
                             + (level.c_west[key] * west[u] + level.c_east[key] * east[u])
                             + level.c_layer[u, b, t] * here[1 - layer][u])
                    yield key, here[layer][u], total


def sweep(level, source, result, blocks):
    for key, value, total in neighbour_sums(level, source, blocks):
        result[key] = (1.0 - damping) * value + level.weight[key] * (level.target[key] + total)


def sweeps(level, count, blocks):
    for _ in range(count):
        sweep(level, level.now, level.later, blocks)
        level.now, level.later = level.later, level.now


def first_sweep(level, blocks):
    for key in level.keys(blocks):
        level.now[key] = level.weight[key] * level.target[key]


def pair_sum(value, span):
    lower = lane_index() % (2 * span) < span
    return value + jnp.where(lower, lane_roll(value, -span), lane_roll(value, span))


def low_group(value, span):
    return jnp.where(lane_index() % (2 * span) < span, value, lane_roll(value, span))


def high_group(value, span):
    return jnp.where(lane_index() % (2 * span) < span, lane_roll(value, -span), value)


def restrict_residual(fine, coarse, blocks):
    partial_sum = {}
    for key, value, total in neighbour_sums(fine, fine.now, blocks):
        layer, u, b, t = key
        residual = fine.target[key] + total - fine.diag[key] * value
        if t % 2 == 0:
            partial_sum[layer, u, b] = residual
        else:
            coarse.target[layer, u, b, t // 2] = pair_sum(partial_sum[layer, u, b] + residual, fine.span)


def prolong(coarse, fine, blocks):
    for key in fine.keys(blocks):
        layer, u, b, t = key
        fine.now[key] = fine.now[key] + coarse.now[layer, u, b, t // 2]


def vcycle(levels, from_zero, blocks):
    finest, middle, bottom = levels
    if from_zero:
        first_sweep(finest, blocks)
    sweeps(finest, SMOOTH - int(from_zero), blocks)
    restrict_residual(finest, middle, blocks)
    first_sweep(middle, blocks)
    sweeps(middle, SMOOTH - 1, blocks)
    restrict_residual(middle, bottom, blocks)
    first_sweep(bottom, blocks)
    sweeps(bottom, COARSE - 1, blocks)
    prolong(bottom, middle, blocks)
    sweeps(middle, SMOOTH, blocks)
    prolong(middle, finest, blocks)
    sweeps(finest, SMOOTH, blocks)


def harmonic(left, right):
    return 2.0 * left * right / jnp.maximum(left + right, 1e-20)


def with_weight(level, key, accumulated):
    layer, u, b, t = key
    diag = (level.c_north[key] + level.c_south[key] + level.c_west[key] + level.c_east[key]
            + level.c_layer[u, b, t] + accumulated)
    level.diag[key] = diag
    level.weight[key] = damping / jnp.maximum(diag, 1e-20)


def coarse_coeffs(fine, coarse, fine_acc, coarse_acc, blocks):
    span = fine.span
    for key in coarse.keys(blocks):
        layer, u, b, t = key
        one, two = (layer, u, b, 2 * t), (layer, u, b, 2 * t + 1)
        coarse.c_north[key] = pair_sum(fine.c_north[one], span)
        coarse.c_south[key] = pair_sum(fine.c_south[two], span)
        coarse.c_west[key] = low_group(fine.c_west[one] + fine.c_west[two], span)
        coarse.c_east[key] = high_group(fine.c_east[one] + fine.c_east[two], span)
        if layer == 0:
            coarse.c_layer[u, b, t] = pair_sum(fine.c_layer[one[1:]] + fine.c_layer[two[1:]], span)
        accumulated = pair_sum(fine_acc[one] + fine_acc[two], span)
        if coarse_acc is not None:
            coarse_acc[key] = accumulated
        with_weight(coarse, key, accumulated)


def cycle_kernel(grid_shape, gx_count, blocks, *refs):
    cells_hbm, rates_hbm = refs[:2]
    inputs = [refs[2 + 2 * b:4 + 2 * b] for b in range(blocks)]
    refs = refs[2 + 2 * blocks:]
    pressure_out, adjoint_out, terms_out = refs[:3]
    refs = refs[3:]
    cells, rates, sems, perm, acc, middle_acc, pressure, pressure_rows, adjoint_rows = refs[:9]
    refs = refs[9:]
    copies = [pltpu.make_async_copy(cells_hbm, cells, sems.at[0]), pltpu.make_async_copy(rates_hbm, rates, sems.at[1])]
    for copy in copies:
        copy.start()
    count = inputs[0][0].shape[2] // SUB
    levels = [Level(count >> depth, 1 << depth, refs[10 * depth:10 * depth + 10]) for depth in range(3)]
    finest, middle, bottom = levels

    def rows(t):
        return pl.ds(t, SUB, stride=count)

    def field(number, key):
        layer, u, b, t = key
        return inputs[b][u][number, layer, rows(t), :]

    gx = lax.axis_index("gx")
    if blocks == 3:
        joined = [1.0, 0.0, 1.0]
    elif blocks == 2:
        joined = [1.0 - gx.astype(jnp.float32), gx.astype(jnp.float32)]
    else:
        joined = [0.0]

    for key in finest.keys(blocks):
        perm[key] = field(PERM, key)
        acc[key] = field(ACC, key)
        start = field(PREV, key)
        finest.now[key] = start
        finest.target[key] = acc[key] * start

    for copy in copies:
        copy.wait()
    layer_count, total_rows, total_cols = grid_shape
    block_rows, block_cols = SUB * count, LANES
    for well in range(WELLS):
        cell = cells[0, well]
        layer = cell // (total_rows * total_cols)
        row = cell // total_cols % total_rows - gx * block_rows
        col = cell % total_cols - lax.axis_index("gy") * block_cols
        if blocks == 3:
            row_inside = (row >= -block_rows) & (row < 2 * block_rows)
        elif blocks == 2:
            row_inside = row >= -block_rows
        else:
            row_inside = row >= 0
        inside = row_inside & (col >= -HALF) & (col < block_cols + HALF)
        row = jnp.where(row < 0, row + blocks * block_rows, row)
        col = jnp.where(col < 0, col + 2 * block_cols, col)
        row = jnp.where(inside, row, 0)
        col = jnp.where(inside, col, 0)
        rate = jnp.where(inside, rates[0, well], 0.0)
        in_block = row % block_rows
        place = layer, col // LANES, row // block_rows, in_block % count
        hit = (row_index() == in_block // count) & (lane_index() == col % LANES)
        finest.target[place] = finest.target[place] + jnp.where(hit, rate, 0.0)

    for layer in range(LAYERS):
        for u in range(2):
            heads = [perm[layer, u, b, 0] for b in range(blocks)]
            edge = row_index() >= SUB - 1
            rolled = [row_roll(value, -1) for value in heads]
            after = [jnp.where(edge, joined[b] * rolled[(b + 1) % blocks], rolled[b]) for b in range(blocks)]
            for b in range(blocks):
                for t in range(count):
                    beyond = perm[layer, u, b, t + 1] if t < count - 1 else after[b]
                    finest.c_south[layer, u, b, t] = harmonic(perm[layer, u, b, t], beyond)
            before = row_before([finest.c_south[layer, u, b, count - 1] for b in range(blocks)], blocks)
            for b in range(blocks):
                for t in range(count):
                    finest.c_north[layer, u, b, t] = finest.c_south[layer, u, b, t - 1] if t > 0 else before[b]
    for b in range(blocks):
        for t in range(count):
            for u in range(2):
                finest.c_layer[u, b, t] = vertical * harmonic(perm[0, u, b, t], perm[1, u, b, t])
            for layer in range(LAYERS):
                here = [perm[layer, u, b, t] for u in range(2)]
                beyond = east_of(here, 1)
                east = [harmonic(here[u], beyond[u]) for u in range(2)]
                west = west_of(east, 1)
                for u in range(2):
                    finest.c_east[layer, u, b, t] = east[u]
                    finest.c_west[layer, u, b, t] = west[u]
    for key in finest.keys(blocks):
        with_weight(finest, key, acc[key])
    coarse_coeffs(finest, middle, acc, middle_acc, blocks)
    coarse_coeffs(middle, bottom, middle_acc, None, blocks)

    vcycle(levels, False, blocks)
    for key in finest.keys(blocks):
        value = finest.now[key]
        pressure[key] = value
        finest.target[key] = value - field(OBS, key)
        layer, u, b, t = key
        if u == 0 and b == 0:
            pressure_rows[0, layer, rows(t), :] = value
    pressure_copy = pltpu.make_async_copy(pressure_rows, pressure_out, sems.at[2])
    pressure_copy.start()
    vcycle(levels, True, blocks)
    for t in range(count):
        for layer in range(LAYERS):
            adjoint_rows[0, layer, rows(t), :] = finest.now[layer, 0, 0, t]
    adjoint_copy = pltpu.make_async_copy(adjoint_rows, adjoint_out, sems.at[3])
    adjoint_copy.start()

    fields = (pressure, finest.now)
    last = count - 1
    ends = {}
    for number, values in enumerate(fields):
        for layer in range(LAYERS):
            ends[number, layer] = (
                row_before([values[layer, 0, b, last] for b in range(blocks)], blocks)[0],
                row_after([values[layer, 0, b, 0] for b in range(blocks)], blocks)[0],
            )
    for t in range(count):
        for layer in range(LAYERS):
            key = layer, 0, 0, t
            differences = []
            for number, values in enumerate(fields):
                pair = [values[layer, u, 0, t] for u in range(2)]
                here = pair[0]
                beside = (
                    values[layer, 0, 0, t - 1] if t > 0 else ends[number, layer][0],
                    values[layer, 0, 0, t + 1] if t < last else ends[number, layer][1],
                    west_of(pair, 1)[0],
                    east_of(pair, 1)[0],
                    values[1 - layer, 0, 0, t],
                )
                differences.append([here - other for other in beside])
            total = jnp.zeros((SUB, LANES), jnp.float32)
            coeffs = (finest.c_north[key], finest.c_south[key], finest.c_west[key], finest.c_east[key])
            for number, coeff in enumerate(coeffs):
                total = total + coeff * coeff * (differences[0][number] * differences[1][number])
            coeff = finest.c_layer[0, 0, t]
            total = total + (1.0 / vertical) * (coeff * coeff) * (differences[0][4] * differences[1][4])
            total = -0.5 * total / perm[key]
            for copy in range(terms_out.shape[0]):
                terms_out[copy, layer, rows(t), :] = total
    pressure_copy.wait()
    adjoint_copy.wait()


def moved(value, axis, step):
    count = lax.axis_size(axis)
    ring = axis == "gx" and count == 2
    pairs = [((i + step) % count, i) for i in range(count) if ring or 0 <= i + step < count]
    return lax.ppermute(value, axis, pairs)


def summed(copies, axis):
    return jnp.sum(lax.all_to_all(copies, axis, 0, 0), 0)


def in_hbm(value):
    return pltpu.with_memory_space_constraint(value, pltpu.HBM)


def in_vmem(value):
    return pltpu.with_memory_space_constraint(value, pltpu.VMEM)


def shards(
    perm_log,
    facies,
    facies_scale,
    accumulation,
    previous_pressure,
    observed,
    well_cells,
    well_rates,
):
    layer_count, row_count, col_count = perm_log.shape
    gx_count, gy_count = lax.axis_size("gx"), lax.axis_size("gy")
    vmem = pl.BlockSpec(memory_space=pltpu.VMEM)
    hbm = pl.BlockSpec(memory_space=pltpu.HBM)
    f32 = jnp.float32
    fields = (perm_log, facies, accumulation, previous_pressure, observed)
    own, to_left, to_right = pl.pallas_call(
        pack_kernel,
        out_shape=[
            pltpu.VMEM((4, layer_count, row_count, col_count), f32),
            pltpu.VMEM((2, layer_count, row_count, col_count), f32),
            pltpu.VMEM((2, layer_count, row_count, col_count), f32),
        ],
        in_specs=[hbm] * 6,
        out_specs=[vmem] * 3,
        scratch_shapes=[pltpu.SMEM(facies_scale.shape, f32)]
        + [pltpu.VMEM(value.shape, value.dtype) for value in fields] + [pltpu.SemaphoreType.DMA((6,))],
        name="pack",
    )(in_hbm(facies_scale), *[in_hbm(value) for value in fields])

    steps = (0, 1) if gx_count == 2 else (0, 1, -1) if gx_count > 2 else (0,)
    blocks = len(steps)
    owns = [own] + [moved(own, "gx", step) for step in steps[1:]]
    beside = pl.pallas_call(
        merge_kernel,
        out_shape=pltpu.VMEM((4, layer_count, row_count, col_count), f32),
        in_specs=[vmem] * 2,
        out_specs=vmem,
        name="merge",
    )(in_vmem(moved(to_left, "gy", 1)), in_vmem(moved(to_right, "gy", -1)))
    besides = [beside] + [moved(beside, "gx", step) for step in steps[1:]]
    operands = [in_vmem(value) for pair in zip(owns, besides) for value in pair]

    count = row_count // SUB
    scratch = [pltpu.SMEM(well_cells.shape, jnp.int32), pltpu.SMEM(well_rates.shape, f32), pltpu.SemaphoreType.DMA((4,))]
    scratch += [pltpu.VMEM((LAYERS, 2, blocks, count, SUB, LANES), f32)] * 2
    scratch += [pltpu.VMEM((LAYERS, 2, blocks, count // 2, SUB, LANES), f32)]
    scratch += [pltpu.VMEM((LAYERS, 2, blocks, count, SUB, LANES), f32)]
    scratch += [pltpu.VMEM((1, layer_count, row_count, col_count), f32)] * 2
    for depth in range(3):
        whole = pltpu.VMEM((LAYERS, 2, blocks, count >> depth, SUB, LANES), f32)
        scratch += [whole] * 4 + [pltpu.VMEM((2, blocks, count >> depth, SUB, LANES), f32)] + [whole] * 5
    state = jax.ShapeDtypeStruct((1, layer_count, row_count, col_count), f32)
    grid_shape = (layer_count, row_count * gx_count, col_count * gy_count)
    pressure, adjoint, terms = pl.pallas_call(
        partial(cycle_kernel, grid_shape, gx_count, blocks),
        out_shape=[state, state, pltpu.VMEM((lax.axis_size("scen"), layer_count, row_count, col_count), f32)],
        in_specs=[hbm] * 2 + [vmem] * (2 * blocks),
        out_specs=[hbm, hbm, vmem],
        scratch_shapes=scratch,
        compiler_params=pltpu.CompilerParams(vmem_limit_bytes=24 * 1024 * 1024),
        name="cycles",
    )(in_hbm(well_cells), in_hbm(well_rates), *operands)
    return pressure, adjoint, summed(terms, "scen")


def solution(mesh):
    return jax.shard_map(
        shards,
        mesh=mesh,
        in_specs=(
            P(None, "gx", "gy"),
            P(None, "gx", "gy"),
            P(),
            P(None, "gx", "gy"),
            P("scen", None, "gx", "gy"),
            P("scen", None, "gx", "gy"),
            P("scen", None),
            P("scen", None),
        ),
        out_specs=(P("scen", None, "gx", "gy"), P("scen", None, "gx", "gy"), P(None, "gx", "gy")),
        check_vma=False,
    )
```

profile of v0, /device:TPU:0, one launch (start us, length us, event | category | flops | bytes accessed | tf_op | source)
XLA Modules:
  0.0 32.6 jit_solution(4755572263125756613)
XLA Ops:
  0.6 1.1 %pack.1 = (f32[4,2,64,128]{3,2,1,0:T(8,128)S(1)}, f32[2,2,64,128]{3,2,1,0:T(8,128)S(1)}, f32[2,2,64,128]{3,2,1,0:T(8,128)S(1)}) custom-call(f32[4]{0:T(128)} %scale_hbm.1, f32[2,64,128]{2,1,0:T(8,128)} %perm_log_hbm.1, s32[2,64,128]{2,1,0:T(8,128)} %facies_hbm.1, f32[2,64,128]{2,1,0:T(8,128)} %acc_hbm.1, f32[1,2,64,128]{3,2,1,0:T(8,128)} %prev_hbm.1, ...), custom_call_target="tpu_custom_call" | custom-call | tf_op jit(solution)/shard_map/pack/pallas_call | solution.py:412
  1.8 1.3 %collective-permute-start = (f32[2,2,64,128]{3,2,1,0:T(8,128)S(1)}, f32[2,2,64,128]{3,2,1,0:T(8,128)S(1)}, u32[]{:S(2)}, u32[]{:S(2)}) collective-permute-start(f32[2,2,64,128]{3,2,1,0:T(8,128)S(1)} %get-tuple-element.10), channel_id=1, source_target_pairs={{1,0},{2,1},{3,2},{5,4},{6,5},{7,6},{9,8},{10,9},{11,10},{13,12},{... | collective-permute-start | bytes 393224 | tf_op jit(solution)/shard_map/ppermute | solution.py:381
  3.1 5.6 %collective-permute-start.1 = (f32[2,2,64,128]{3,2,1,0:T(8,128)S(1)}, f32[2,2,64,128]{3,2,1,0:T(8,128)S(1)}, u32[]{:S(2)}, u32[]{:S(2)}) collective-permute-start(f32[2,2,64,128]{3,2,1,0:T(8,128)S(1)} %get-tuple-element.11), channel_id=1, source_target_pairs={{0,1},{1,2},{2,3},{4,5},{5,6},{6,7},{8,9},{9,10},{10,11},{12,13},{... | collective-permute-start | bytes 393224 | tf_op jit(solution)/shard_map/ppermute | solution.py:381
  8.6 0.1 collective-permute-start.2
  8.7 1.5 %collective-permute-done.from_right = f32[2,2,64,128]{3,2,1,0:T(8,128)S(1)} collective-permute-done((f32[2,2,64,128]{3,2,1,0:T(8,128)S(1)}, f32[2,2,64,128]{3,2,1,0:T(8,128)S(1)}, u32[]{:S(2)}, u32[]{:S(2)}) %collective-permute-start) | collective-permute-done | bytes 131104 | tf_op jit(solution)/shard_map/ppermute | solution.py:381
  10.2 1.2 %collective-permute-done.1.from_left = f32[2,2,64,128]{3,2,1,0:T(8,128)S(1)} collective-permute-done((f32[2,2,64,128]{3,2,1,0:T(8,128)S(1)}, f32[2,2,64,128]{3,2,1,0:T(8,128)S(1)}, u32[]{:S(2)}, u32[]{:S(2)}) %collective-permute-start.1) | collective-permute-done | bytes 131104 | tf_op jit(solution)/shard_map/ppermute | solution.py:381
  11.4 0.1 merge.1.refs_3_
  11.5 0.1 collective-permute-start.3
  11.6 0.0 collective-permute-done.2.refs_4_
  11.6 1.5 %collective-permute-done.3.refs_5_ = f32[4,2,64,128]{3,2,1,0:T(8,128)S(1)} collective-permute-done((f32[4,2,64,128]{3,2,1,0:T(8,128)S(1)}, f32[4,2,64,128]{3,2,1,0:T(8,128)S(1)}, u32[]{:S(2)}, u32[]{:S(2)}) %collective-permute-start.3) | collective-permute-done | bytes 262176 | tf_op jit(solution)/shard_map/ppermute | solution.py:381
  13.1 9.1 %cycles.1 = (f32[1,2,64,128]{3,2,1,0:T(8,128)}, f32[1,2,64,128]{3,2,1,0:T(8,128)}, f32[4,2,64,128]{3,2,1,0:T(8,128)S(1)}) custom-call(s32[1,5]{1,0:T(1,128)} %refs_0_.1, f32[1,5]{1,0:T(1,128)} %refs_1_.1, f32[4,2,64,128]{3,2,1,0:T(8,128)S(1)} %get-tuple-element.9.refs_2_, f32[4,2,64,128]{3,2,1,0:T(8,128)S(1)} %merge.1.refs_3_, ...), custom_call_target="tpu_custom_call" | custom-call | tf_op jit(solution)/shard_map/cycles/pallas_call | solution.py:450
  22.2 9.7 %all_to_all.5 = f32[4,2,64,128]{3,2,1,0:T(8,128)S(1)} all-to-all(f32[4,2,64,128]{3,2,1,0:T(8,128)S(1)} %get-tuple-element.14), channel_id=1, replica_groups=mesh['scen'=4,'gx'=2,'gy'=4] {'scen'}, dimensions={0} | all-to-all | bytes 524288 | tf_op jit(solution)/shard_map/all_to_all | solution.py:385
  32.0 0.6 %reduce_sum.9 = f32[2,64,128]{2,1,0:T(8,128)} reduce(f32[4,2,64,128]{3,2,1,0:T(8,128)S(1)} %all_to_all.5, f32[]{:T(128)} %constant.0.clone.1), dimensions={0}, to_apply=%region_0.0 | reduce | flops 49152 | bytes 327684 | tf_op jit(solution)/shard_map/reduce_sum | solution.py:385
Async XLA Ops:
  1.8 8.4 %collective-permute-start = (f32[2,2,64,128]{3,2,1,0:T(8,128)S(1)}, f32[2,2,64,128]{3,2,1,0:T(8,128)S(1)}, u32[]{:S(2)}, u32[]{:S(2)}) collective-permute-start(f32[2,2,64,128]{3,2,1,0:T(8,128)S(1)} %get-tuple-element.10), channel_id=1, source_target_pairs={{1,0},{2,1},{3,2},{5,4},{6,5},{7,6},{9,8},{10,9},{11,10},{13,12},{... | collective-permute-start | bytes 393224 | tf_op jit(solution)/shard_map/ppermute | solution.py:381
  3.1 8.3 %collective-permute-start.1 = (f32[2,2,64,128]{3,2,1,0:T(8,128)S(1)}, f32[2,2,64,128]{3,2,1,0:T(8,128)S(1)}, u32[]{:S(2)}, u32[]{:S(2)}) collective-permute-start(f32[2,2,64,128]{3,2,1,0:T(8,128)S(1)} %get-tuple-element.11), channel_id=1, source_target_pairs={{0,1},{1,2},{2,3},{4,5},{5,6},{6,7},{8,9},{9,10},{10,11},{12,13},{... | collective-permute-start | bytes 393224 | tf_op jit(solution)/shard_map/ppermute | solution.py:381
  8.6 2.9 %collective-permute-start.2 = (f32[4,2,64,128]{3,2,1,0:T(8,128)S(1)}, f32[4,2,64,128]{3,2,1,0:T(8,128)S(1)}, u32[]{:S(2)}, u32[]{:S(2)}) collective-permute-start(f32[4,2,64,128]{3,2,1,0:T(8,128)S(1)} %get-tuple-element.9.refs_2_), channel_id=1, source_target_pairs={{4,0},{0,4},{5,1},{1,5},{6,2},{2,6},{7,3},{3,7},{12,8},{8,12},{13,... | collective-permute-start | bytes 786440 | tf_op jit(solution)/shard_map/ppermute | solution.py:381
  11.5 1.6 %collective-permute-start.3 = (f32[4,2,64,128]{3,2,1,0:T(8,128)S(1)}, f32[4,2,64,128]{3,2,1,0:T(8,128)S(1)}, u32[]{:S(2)}, u32[]{:S(2)}) collective-permute-start(f32[4,2,64,128]{3,2,1,0:T(8,128)S(1)} %merge.1.refs_3_), channel_id=1, source_target_pairs={{4,0},{0,4},{5,1},{1,5},{6,2},{2,6},{7,3},{3,7},{12,8},{8,12},{13,... | collective-permute-start | bytes 786440 | tf_op jit(solution)/shard_map/ppermute | solution.py:381
where the time goes:
time: 32.9 us; the launch traced here: 32.6 us
  Pallas kernels  10.4 us (32%)
  blocking collectives  9.73 us (30%)
  starting transfers between devices  7 us (21%)
  waiting for transfers between devices  4.16 us (13%)
  between operations  0.7 us (2%)
  other arithmetic  0.64 us (2%)
    all_to_all x1, blocking collectives, summed(): return jnp.sum(lax.all_to_all(copies, axis, 0, 0), 0)  9.73 us
    pallas_call x1, Pallas kernels, shards(): pl.pallas_call(partial(cycle_kernel, grid_shape, gx_count, blocks), out_s...  9.15 us
    ppermute x4, starting transfers between devices, moved(): return lax.ppermute(value, axis, pairs)  7 us
    ppermute x4, waiting for transfers between devices, moved(): return lax.ppermute(value, axis, pairs)  4.16 us
    pallas_call x1, Pallas kernels, shards(): pl.pallas_call(pack_kernel, out_shape=[pltpu.VMEM((4, layer_count, row_co...  1.12 us
  transfers between devices with their start and end apart: 4, of which 3 were waited for; matrix products, arithmetic and copies ran while one was open for 0% of the time, Pallas kernels for 0%

commit v1 on v0

v1 whole, which is shorter than its diff:
```python
from functools import partial

import jax
import jax.numpy as jnp
from jax import lax
from jax.experimental import pallas as pl
from jax.experimental.pallas import tpu as pltpu
from jax.sharding import PartitionSpec as P

WELLS = 5
FACIES = 4
LAYERS = 2
SMOOTH = 2
COARSE = 4

vertical = 0.3
damping = 0.8

LANES = 128
HALF = 64
SUB = 8
PERM, ACC, PREV, OBS = range(4)
LEVELS = ((2, 1), (1, 1), (1, 2))


def lane_index():
    return lax.broadcasted_iota(jnp.int32, (SUB, LANES), 1)


def row_index():
    return lax.broadcasted_iota(jnp.int32, (SUB, LANES), 0)


def lane_roll(value, shift):
    return pltpu.roll(value, shift % LANES, value.ndim - 1)


def row_roll(value, shift):
    return pltpu.roll(value, shift % SUB, 0)


def shuffle(value, inverse):
    rows = lax.broadcasted_iota(jnp.int32, (LANES, LANES), 0)
    cols = lax.broadcasted_iota(jnp.int32, (LANES, LANES), 1)
    natural, place = (cols, rows) if inverse else (rows, cols)
    matrix = (natural == 2 * (place % HALF) + place // HALF).astype(jnp.float32)
    flat = value.reshape(-1, LANES)
    moved_columns = lax.dot(flat, matrix, precision=lax.Precision.HIGHEST, preferred_element_type=jnp.float32)
    return moved_columns.reshape(value.shape)


def pack_kernel(scale_hbm, perm_log_hbm, facies_hbm, acc_hbm, prev_hbm, obs_hbm, own, to_left, to_right,
                scale, perm_log, facies, acc, prev, obs, sems):
    pairs = ((scale_hbm, scale), (perm_log_hbm, perm_log), (facies_hbm, facies), (acc_hbm, acc), (prev_hbm, prev),
             (obs_hbm, obs))
    copies = [pltpu.make_async_copy(source, target, sems.at[i]) for i, (source, target) in enumerate(pairs)]
    for copy in copies:
        copy.start()
    for copy in copies:
        copy.wait()
    label = facies[...]
    factor = jnp.zeros(label.shape, jnp.float32)
    for number in range(FACIES):
        factor = factor + jnp.where(label == number, scale[number], jnp.float32(0.0))
    fields = [shuffle(value, False) for value in (jnp.exp(perm_log[...]) * factor, acc[...], prev[0], obs[0])]
    low = lax.broadcasted_iota(jnp.int32, label.shape, 2) % HALF < HALF // 2
    for number in range(4):
        own[number] = fields[number]
    for pair in range(2):
        first = lane_roll(fields[2 * pair], HALF)
        second = lane_roll(fields[2 * pair + 1], HALF + HALF // 2)
        to_left[pair] = jnp.where(low, first, second)
        to_right[pair] = jnp.where(low, second, first)


def merge_kernel(from_right, from_left, beside):
    low = lax.broadcasted_iota(jnp.int32, beside.shape[1:], 2) % HALF < HALF // 2
    for pair in range(2):
        right, left = from_right[pair], from_left[pair]
        beside[2 * pair] = jnp.where(low, right, left)
        beside[2 * pair + 1] = lane_roll(jnp.where(low, left, right), -(HALF // 2))


class Level:
    def __init__(self, count, width, span, blocks, refs):
        self.count = count
        self.width = width
        self.span = span
        self.blocks = blocks
        (self.c_south, self.c_first, self.c_inner, self.c_east, self.c_west, self.c_layer, self.weight, self.diag,
         self.target, self.now, self.later) = refs

    @staticmethod
    def scratch(count, width, blocks):
        def vectors(*lead):
            return pltpu.VMEM(lead + (SUB, LANES), jnp.float32)

        whole = vectors(LAYERS, width, blocks, count)
        edge = vectors(LAYERS, blocks, count)
        return [whole, vectors(LAYERS, width, blocks), edge, edge, edge, vectors(width, blocks, count)] + [whole] * 5

    def steps(self, ring=None):
        for b in range(self.blocks):
            for t in range(self.count):
                if ring is None or b == 0 or t < ring or t >= self.count - ring:
                    yield b, t

    def members(self):
        for layer in range(LAYERS):
            for u in range(self.width):
                yield layer, u


def row_before(values):
    edge = row_index() < 1
    rolled = [row_roll(value, 1) for value in values]
    return [jnp.where(edge, rolled[b - 1], rolled[b]) for b in range(len(values))]


def row_after(values):
    edge = row_index() >= SUB - 1
    rolled = [row_roll(value, -1) for value in values]
    return [jnp.where(edge, rolled[(b + 1) % len(values)], rolled[b]) for b in range(len(values))]


class Field:
    def __init__(self, level, source):
        self.source = source
        self.count = level.count
        self.read = {}
        self.before, self.after = {}, {}
        for layer, u in level.members():
            lows = row_before([source[layer, u, b, level.count - 1] for b in range(level.blocks)])
            highs = row_after([source[layer, u, b, 0] for b in range(level.blocks)])
            for b in range(level.blocks):
                self.before[layer, u, b] = lows[b]
                self.after[layer, u, b] = highs[b]

    def at(self, layer, u, b, t):
        if t < 0:
            return self.before[layer, u, b]
        if t >= self.count:
            return self.after[layer, u, b]
        key = layer, u, b, t
        if key not in self.read:
            self.read[key] = self.source[key]
        return self.read[key]


def row_coeff(level, layer, u, b, t):
    return level.c_south[layer, u, b, t] if t >= 0 else level.c_first[layer, u, b]


def neighbour_sums(level, source, ring=None):
    field = Field(level, source)
    coeffs = {}
    for b, t in level.steps(ring):
        for member in level.members():
            for at in (t - 1, t):
                if (member, b, at) not in coeffs:
                    coeffs[member, b, at] = row_coeff(level, *member, b, at)
        layer_coeffs = [level.c_layer[u, b, t] for u in range(level.width)]
        for layer in range(LAYERS):
            here = [field.at(layer, u, b, t) for u in range(level.width)]
            east_coeff, west_coeff = level.c_east[layer, b, t], level.c_west[layer, b, t]
            if level.width == 2:
                inner = level.c_inner[layer, b, t]
                beside = [inner * here[1] + west_coeff * lane_roll(here[1], 1),
                          inner * here[0] + east_coeff * lane_roll(here[0], -1)]
            else:
                beside = [east_coeff * lane_roll(here[0], -level.span) + west_coeff * lane_roll(here[0], level.span)]
            for u in range(level.width):
                total = (coeffs[(layer, u), b, t - 1] * field.at(layer, u, b, t - 1)
                         + coeffs[(layer, u), b, t] * field.at(layer, u, b, t + 1)
                         + (beside[u] + layer_coeffs[u] * field.at(1 - layer, u, b, t)))
                yield (layer, u, b, t), here[u], total


def sweep(level, source, result, ring=None):
    for key, value, total in neighbour_sums(level, source, ring):
        result[key] = (1.0 - damping) * value + level.weight[key] * (level.target[key] + total)


def sweeps(level, count, ring=None):
    for number in range(count):
        sweep(level, level.now, level.later, None if ring is None else ring + count - 1 - number)
        level.now, level.later = level.later, level.now


def first_sweep(level):
    for b, t in level.steps():
        for layer, u in level.members():
            key = layer, u, b, t
            level.now[key] = level.weight[key] * level.target[key]


def pair_sum(value, span):
    lower = lane_index() % (2 * span) < span
    return value + jnp.where(lower, lane_roll(value, -span), lane_roll(value, span))


def low_group(value, span):
    return jnp.where(lane_index() % (2 * span) < span, value, lane_roll(value, span))


def high_group(value, span):
    return jnp.where(lane_index() % (2 * span) < span, lane_roll(value, -span), value)


def column_sum(values, level):
    return values[0] + values[1] if level.width == 2 else pair_sum(values[0], level.span)


def restrict_residual(fine, coarse):
    residuals = {}
    for key, value, total in neighbour_sums(fine, fine.now):
        layer, u, b, t = key
        residuals[key] = fine.target[key] + total - fine.diag[key] * value
        if t % 2 == 1 and u == fine.width - 1:
            rows = [residuals[layer, v, b, t - 1] + residuals[layer, v, b, t] for v in range(fine.width)]
            coarse.target[layer, 0, b, t // 2] = column_sum(rows, fine)


def prolong(coarse, fine, ring=None):
    for b, t in fine.steps(ring):
        for layer, u in fine.members():
            key = layer, u, b, t
            fine.now[key] = fine.now[key] + coarse.now[layer, 0, b, t // 2]


def vcycle(levels, from_zero, ring=None):
    finest, middle, bottom = levels
    if from_zero:
        first_sweep(finest)
    sweeps(finest, SMOOTH - int(from_zero))
    restrict_residual(finest, middle)
    first_sweep(middle)
    sweeps(middle, SMOOTH - 1)
    restrict_residual(middle, bottom)
    first_sweep(bottom)
    sweeps(bottom, COARSE - 1)
    prolong(bottom, middle)
    sweeps(middle, SMOOTH)
    prolong(middle, finest, None if ring is None else ring + SMOOTH)
    sweeps(finest, SMOOTH, ring)


def harmonic(left, right):
    return 2.0 * left * right / jnp.maximum(left + right, 1e-20)


def finest_coeffs(level, perm, joined):
    last = level.count - 1
    for layer, u in level.members():
        heads = [perm[layer, u, b, 0] for b in range(level.blocks)]
        rolled = [row_roll(value, -1) for value in heads]
        edge = row_index() >= SUB - 1
        for b in range(level.blocks):
            after = jnp.where(edge, joined[b] * rolled[(b + 1) % level.blocks], rolled[b])
            for t in range(level.count):
                beyond = perm[layer, u, b, t + 1] if t < last else after
                level.c_south[layer, u, b, t] = harmonic(perm[layer, u, b, t], beyond)
        firsts = row_before([level.c_south[layer, u, b, last] for b in range(level.blocks)])
        for b in range(level.blocks):
            level.c_first[layer, u, b] = firsts[b]
    for b, t in level.steps():
        for u in range(level.width):
            level.c_layer[u, b, t] = vertical * harmonic(perm[0, u, b, t], perm[1, u, b, t])
        for layer in range(LAYERS):
            even, odd = perm[layer, 0, b, t], perm[layer, 1, b, t]
            level.c_inner[layer, b, t] = harmonic(even, odd)
            east = harmonic(odd, lane_roll(even, -1))
            level.c_east[layer, b, t] = east
            level.c_west[layer, b, t] = lane_roll(east, 1)


def with_weight(level, acc):
    for b, t in level.steps():
        for layer, u in level.members():
            key = layer, u, b, t
            if level.width == 2:
                beside = level.c_inner[layer, b, t] + (level.c_west, level.c_east)[u][layer, b, t]
            else:
                beside = level.c_west[layer, b, t] + level.c_east[layer, b, t]
            diag = (row_coeff(level, layer, u, b, t - 1) + row_coeff(level, layer, u, b, t)
                    + (beside + level.c_layer[u, b, t]) + acc[key])
            level.diag[key] = diag
            level.weight[key] = damping / jnp.maximum(diag, 1e-20)


def coarse_coeffs(fine, coarse, fine_acc, coarse_acc):
    width = range(fine.width)
    for b in range(coarse.blocks):
        for layer in range(LAYERS):
            coarse.c_first[layer, 0, b] = column_sum([fine.c_first[layer, u, b] for u in width], fine)
    for b, t in coarse.steps():
        one, two = 2 * t, 2 * t + 1
        coarse.c_layer[0, b, t] = column_sum([fine.c_layer[u, b, one] + fine.c_layer[u, b, two] for u in width], fine)
        for layer in range(LAYERS):
            coarse.c_south[layer, 0, b, t] = column_sum([fine.c_south[layer, u, b, two] for u in width], fine)
            coarse_acc[layer, 0, b, t] = column_sum(
                [fine_acc[layer, u, b, one] + fine_acc[layer, u, b, two] for u in width], fine)
            west = fine.c_west[layer, b, one] + fine.c_west[layer, b, two]
            east = fine.c_east[layer, b, one] + fine.c_east[layer, b, two]
            if fine.width == 1:
                west, east = low_group(west, fine.span), high_group(east, fine.span)
            coarse.c_west[layer, b, t] = west
            coarse.c_east[layer, b, t] = east
    with_weight(coarse, coarse_acc)


def own_columns(even, odd):
    return jnp.where(lane_index() < HALF, even, lane_roll(odd, HALF))


def face_terms(level, pressure, adjoint, perm):
    def face(coeff, one, two):
        changes = [field.at(*one) - (field.at(*two) if isinstance(two, tuple) else two[number])
                   for number, field in enumerate((pressure, adjoint))]
        return (coeff * coeff) * (changes[0] * changes[1])

    rows = {(layer, u): face(level.c_first[layer, u, 0], (layer, u, 0, -1), (layer, u, 0, 0))
            for layer, u in level.members()}
    for t in range(level.count):
        between = [(1.0 / vertical) * face(level.c_layer[u, 0, t], (0, u, 0, t), (1, u, 0, t)) for u in range(2)]
        for layer in range(LAYERS):
            inner = face(level.c_inner[layer, 0, t], (layer, 0, 0, t), (layer, 1, 0, t))
            easts = [lane_roll(field.at(layer, 0, 0, t), -1) for field in (pressure, adjoint)]
            east = face(level.c_east[layer, 0, t], (layer, 1, 0, t), easts)
            terms = []
            for u in range(2):
                south = face(level.c_south[layer, u, 0, t], (layer, u, 0, t), (layer, u, 0, t + 1))
                beside = lane_roll(east, 1) if u == 0 else east
                total = rows[layer, u] + south + (inner + beside) + between[u]
                rows[layer, u] = south
                terms.append(-0.5 * total / perm[layer, u, 0, t])
            yield layer, t, own_columns(*terms)


def cycle_kernel(grid_shape, blocks, *refs):
    cells_hbm, rates_hbm = refs[:2]
    inputs = [refs[2 + 2 * b:4 + 2 * b] for b in range(blocks)]
    refs = refs[2 + 2 * blocks:]
    pressure_out, adjoint_out, terms_out = refs[:3]
    cells, rates, sems, perm, acc, middle_acc, bottom_acc, pressure, pressure_rows, adjoint_rows, terms_rows = refs[3:14]
    refs = refs[14:]
    copies = [pltpu.make_async_copy(cells_hbm, cells, sems.at[0]), pltpu.make_async_copy(rates_hbm, rates, sems.at[1])]
    for copy in copies:
        copy.start()
    count = inputs[0][0].shape[2] // SUB
    levels = [Level(count >> depth, width, span, blocks, refs[11 * depth:11 * depth + 11])
              for depth, (width, span) in enumerate(LEVELS)]
    finest, middle, bottom = levels

    def rows(t):
        return pl.ds(t, SUB, stride=count)

    def fields(number, layer, b, t):
        low = lane_index() < HALF
        own, beside = [value[number, layer, rows(t), :] for value in inputs[b]]
        return jnp.where(low, own, beside), lane_roll(jnp.where(low, beside, own), HALF)

    gx = lax.axis_index("gx")
    if blocks == 3:
        joined = [1.0, 0.0, 1.0]
    elif blocks == 2:
        joined = [1.0 - gx.astype(jnp.float32), gx.astype(jnp.float32)]
    else:
        joined = [0.0]

    for b, t in finest.steps():
        for layer in range(LAYERS):
            perms, accs, starts = [fields(number, layer, b, t) for number in (PERM, ACC, PREV)]
            for u in range(2):
                key = layer, u, b, t
                perm[key] = perms[u]
                acc[key] = accs[u]
                finest.now[key] = starts[u]
                finest.target[key] = accs[u] * starts[u]

    for copy in copies:
        copy.wait()
    layer_count, total_rows, total_cols = grid_shape
    block_rows, block_cols = SUB * count, LANES
    for well in range(WELLS):
        cell = cells[0, well]
        layer = cell // (total_rows * total_cols)
        row = cell // total_cols % total_rows - gx * block_rows
        col = cell % total_cols - lax.axis_index("gy") * block_cols
        if blocks == 3:
            row_inside = (row >= -block_rows) & (row < 2 * block_rows)
        elif blocks == 2:
            row_inside = row >= -block_rows
        else:
            row_inside = row >= 0
        inside = row_inside & (col >= -HALF) & (col < block_cols + HALF)
        row = jnp.where(row < 0, row + blocks * block_rows, row)
        col = jnp.where(col < 0, col + 2 * block_cols, col)
        row = jnp.where(inside, row, 0)
        col = jnp.where(inside, col, 0)
        rate = jnp.where(inside, rates[0, well], 0.0)
        in_block = row % block_rows
        place = layer, col % 2, row // block_rows, in_block % count
        hit = (row_index() == in_block // count) & (lane_index() == col // 2)
        finest.target[place] = finest.target[place] + jnp.where(hit, rate, 0.0)

    finest_coeffs(finest, perm, joined)
    with_weight(finest, acc)
    coarse_coeffs(finest, middle, acc, middle_acc)
    coarse_coeffs(middle, bottom, middle_acc, bottom_acc)

    vcycle(levels, False)
    for b, t in finest.steps():
        for layer in range(LAYERS):
            observed = fields(OBS, layer, b, t)
            values = []
            for u in range(2):
                key = layer, u, b, t
                values.append(finest.now[key])
                pressure[key] = values[u]
                finest.target[key] = values[u] - observed[u]
            if b == 0:
                pressure_rows[0, layer, rows(t), :] = own_columns(*values)
    pressure_rows[...] = shuffle(pressure_rows[...], True)
    pressure_copy = pltpu.make_async_copy(pressure_rows, pressure_out, sems.at[2])
    pressure_copy.start()
    vcycle(levels, True, 1)
    for t in range(count):
        for layer in range(LAYERS):
            adjoint_rows[0, layer, rows(t), :] = own_columns(*[finest.now[layer, u, 0, t] for u in range(2)])
    adjoint_rows[...] = shuffle(adjoint_rows[...], True)
    adjoint_copy = pltpu.make_async_copy(adjoint_rows, adjoint_out, sems.at[3])
    adjoint_copy.start()

    for layer, t, terms in face_terms(finest, Field(finest, pressure), Field(finest, finest.now), perm):
        terms_rows[layer, rows(t), :] = terms
    terms_out[...] = shuffle(terms_rows[...], True)
    pressure_copy.wait()
    adjoint_copy.wait()


def moved(value, axis, step):
    count = lax.axis_size(axis)
    ring = axis == "gx" and count == 2
    pairs = [((i + step) % count, i) for i in range(count) if ring or 0 <= i + step < count]
    return lax.ppermute(value, axis, pairs)


def summed(value, axis):
    count = lax.axis_size(axis)
    others = [lax.ppermute(value, axis, [(i, i ^ step) for i in range(count)]) for step in range(1, count)]
    terms = [value] + others
    while len(terms) > 1:
        terms = [terms[i] + terms[i + 1] for i in range(0, len(terms), 2)]
    return terms[0]


def in_hbm(value):
    return pltpu.with_memory_space_constraint(value, pltpu.HBM)


def in_vmem(value):
    return pltpu.with_memory_space_constraint(value, pltpu.VMEM)


def shards(
    perm_log,
    facies,
    facies_scale,
    accumulation,
    previous_pressure,
    observed,
    well_cells,
    well_rates,
):
    layer_count, row_count, col_count = perm_log.shape
    gx_count, gy_count = lax.axis_size("gx"), lax.axis_size("gy")
    vmem = pl.BlockSpec(memory_space=pltpu.VMEM)
    hbm = pl.BlockSpec(memory_space=pltpu.HBM)
    f32 = jnp.float32
    fields = (perm_log, facies, accumulation, previous_pressure, observed)
    own, to_left, to_right = pl.pallas_call(
        pack_kernel,
        out_shape=[
            pltpu.VMEM((4, layer_count, row_count, col_count), f32),
            pltpu.VMEM((2, layer_count, row_count, col_count), f32),
            pltpu.VMEM((2, layer_count, row_count, col_count), f32),
        ],
        in_specs=[hbm] * 6,
        out_specs=[vmem] * 3,
        scratch_shapes=[pltpu.SMEM(facies_scale.shape, f32)]
        + [pltpu.VMEM(value.shape, value.dtype) for value in fields] + [pltpu.SemaphoreType.DMA((6,))],
        name="pack",
    )(in_hbm(facies_scale), *[in_hbm(value) for value in fields])

    steps = (0, 1) if gx_count == 2 else (0, 1, -1) if gx_count > 2 else (0,)
    blocks = len(steps)
    owns = [own] + [moved(own, "gx", step) for step in steps[1:]]
    beside = pl.pallas_call(
        merge_kernel,
        out_shape=pltpu.VMEM((4, layer_count, row_count, col_count), f32),
        in_specs=[vmem] * 2,
        out_specs=vmem,
        name="merge",
    )(in_vmem(moved(to_left, "gy", 1)), in_vmem(moved(to_right, "gy", -1)))
    besides = [beside] + [moved(beside, "gx", step) for step in steps[1:]]
    operands = [in_vmem(value) for pair in zip(owns, besides) for value in pair]

    count = row_count // SUB
    block = (layer_count, row_count, col_count)
    scratch = [pltpu.SMEM(well_cells.shape, jnp.int32), pltpu.SMEM(well_rates.shape, f32), pltpu.SemaphoreType.DMA((4,))]
    whole = [pltpu.VMEM((LAYERS, width, blocks, count >> depth, SUB, LANES), f32) for depth, (width, _) in enumerate(LEVELS)]
    scratch += [whole[0], whole[0], whole[1], whole[2], whole[0]]
    scratch += [pltpu.VMEM((1,) + block, f32)] * 2 + [pltpu.VMEM(block, f32)]
    for depth, (width, _) in enumerate(LEVELS):
        scratch += Level.scratch(count >> depth, width, blocks)
    state = jax.ShapeDtypeStruct((1, layer_count, row_count, col_count), f32)
    grid_shape = (layer_count, row_count * gx_count, col_count * gy_count)
    pressure, adjoint, terms = pl.pallas_call(
        partial(cycle_kernel, grid_shape, blocks),
        out_shape=[state, state, pltpu.VMEM(block, f32)],
        in_specs=[hbm] * 2 + [vmem] * (2 * blocks),
        out_specs=[hbm, hbm, vmem],
        scratch_shapes=scratch,
        compiler_params=pltpu.CompilerParams(vmem_limit_bytes=24 * 1024 * 1024),
        name="cycles",
    )(in_hbm(well_cells), in_hbm(well_rates), *operands)
    return pressure, adjoint, summed(terms, "scen")


def solution(mesh):
    return jax.shard_map(
        shards,
        mesh=mesh,
        in_specs=(
            P(None, "gx", "gy"),
            P(None, "gx", "gy"),
            P(),
            P(None, "gx", "gy"),
            P("scen", None, "gx", "gy"),
            P("scen", None, "gx", "gy"),
            P("scen", None),
            P("scen", None),
        ),
        out_specs=(P("scen", None, "gx", "gy"), P("scen", None, "gx", "gy"), P(None, "gx", "gy")),
        check_vma=False,
    )
```

time: 32.9 us -> 26.1 us (0.79)
  blocking collectives: 9.73 us -> 0 us
  Pallas kernels: 10.4 us -> 5.92 us
  waiting for transfers between devices: 4.16 us -> 8.1 us
  starting transfers between devices: 7 us -> 10.6 us
    all_to_all x1 -> x0, blocking collectives: 9.73 us -> none  [summed(): return jnp.sum(lax.all_to_all(copies, axis, 0, 0), 0)]
    pallas_call x1, Pallas kernels: 9.15 us -> 4.33 us  [shards(): pl.pallas_call(partial(cycle_kernel, grid_shape, blocks), out_shape=[stat...]
    ppermute x0 -> x3, waiting for transfers between devices: none -> 3.93 us  [summed(): lax.ppermute(value, axis, [(i, i ^ step) for i in range(count)])]
    ppermute x0 -> x3, starting transfers between devices: none -> 3.55 us  [summed(): lax.ppermute(value, axis, [(i, i ^ step) for i in range(count)])]
    add x0 -> x1, other arithmetic: none -> 0.65 us  [summed(): terms = [terms[i] + terms[i + 1] for i in range(0, len(terms), 2)]]
    reduce_sum x1 -> x0, other arithmetic: 0.64 us -> none  [summed(): return jnp.sum(lax.all_to_all(copies, axis, 0, 0), 0)]
    pallas_call x1, Pallas kernels: 1.12 us -> 1.5 us  [shards(): pl.pallas_call(pack_kernel, out_shape=[pltpu.VMEM((4, layer_count, row_co...]
  transfers between devices with their start and end apart: 4 -> 7, of which waited for: 3 -> 6; matrix products, arithmetic and copies ran while one was open for 0% -> 0% of each run, Pallas kernels for 0% -> 0%
where the time goes in v1:
time: 26.1 us; the launch traced here: 25.9 us
  starting transfers between devices  10.6 us (41%)
  waiting for transfers between devices  8.1 us (31%)
  Pallas kernels  5.92 us (23%)
  between operations  0.7 us (3%)
  other arithmetic  0.65 us (2%)
    ppermute x4, starting transfers between devices, moved(): return lax.ppermute(value, axis, pairs)  7 us
    pallas_call x1, Pallas kernels, shards(): pl.pallas_call(partial(cycle_kernel, grid_shape, blocks), out_shape=[stat...  4.33 us
    ppermute x4, waiting for transfers between devices, moved(): return lax.ppermute(value, axis, pairs)  4.16 us
    ppermute x3, waiting for transfers between devices, summed(): lax.ppermute(value, axis, [(i, i ^ step) for i in range(count)])  3.93 us
    ppermute x3, starting transfers between devices, summed(): lax.ppermute(value, axis, [(i, i ^ step) for i in range(count)])  3.55 us
    pallas_call x1, Pallas kernels, shards(): pl.pallas_call(pack_kernel, out_shape=[pltpu.VMEM((4, layer_count, row_co...  1.5 us
    add x1, other arithmetic, summed(): terms = [terms[i] + terms[i + 1] for i in range(0, len(terms), 2)]  0.65 us
  transfers between devices with their start and end apart: 7, of which 6 were waited for; matrix products, arithmetic and copies ran while one was open for 0% of the time, Pallas kernels for 0%

profile of v1, /device:TPU:0, one launch (start us, length us, event | category | flops | bytes accessed | tf_op | source)
XLA Modules:
  0.0 25.9 jit_solution(408046038900312643)
XLA Ops:
  0.6 1.5 %pack.1 = (f32[4,2,64,128]{3,2,1,0:T(8,128)S(1)}, f32[2,2,64,128]{3,2,1,0:T(8,128)S(1)}, f32[2,2,64,128]{3,2,1,0:T(8,128)S(1)}) custom-call(f32[4]{0:T(128)} %scale_hbm.1, f32[2,64,128]{2,1,0:T(8,128)} %perm_log_hbm.1, s32[2,64,128]{2,1,0:T(8,128)} %facies_hbm.1, f32[2,64,128]{2,1,0:T(8,128)} %acc_hbm.1, f32[1,2,64,128]{3,2,1,0:T(8,128)} %prev_hbm.1, ...), custom_call_target="tpu_custom_call" | custom-call | tf_op jit(solution)/shard_map/pack/pallas_call | solution.py:482
  2.1 1.3 %collective-permute-start = (f32[2,2,64,128]{3,2,1,0:T(8,128)S(1)}, f32[2,2,64,128]{3,2,1,0:T(8,128)S(1)}, u32[]{:S(2)}, u32[]{:S(2)}) collective-permute-start(f32[2,2,64,128]{3,2,1,0:T(8,128)S(1)} %get-tuple-element.10), channel_id=1, source_target_pairs={{1,0},{2,1},{3,2},{5,4},{6,5},{7,6},{9,8},{10,9},{11,10},{13,12},{... | collective-permute-start | bytes 393224 | tf_op jit(solution)/shard_map/ppermute | solution.py:446
  3.4 5.6 %collective-permute-start.1 = (f32[2,2,64,128]{3,2,1,0:T(8,128)S(1)}, f32[2,2,64,128]{3,2,1,0:T(8,128)S(1)}, u32[]{:S(2)}, u32[]{:S(2)}) collective-permute-start(f32[2,2,64,128]{3,2,1,0:T(8,128)S(1)} %get-tuple-element.11), channel_id=1, source_target_pairs={{0,1},{1,2},{2,3},{4,5},{5,6},{6,7},{8,9},{9,10},{10,11},{12,13},{... | collective-permute-start | bytes 393224 | tf_op jit(solution)/shard_map/ppermute | solution.py:446
  9.0 0.1 collective-permute-start.2
  9.1 1.5 %collective-permute-done.from_right = f32[2,2,64,128]{3,2,1,0:T(8,128)S(1)} collective-permute-done((f32[2,2,64,128]{3,2,1,0:T(8,128)S(1)}, f32[2,2,64,128]{3,2,1,0:T(8,128)S(1)}, u32[]{:S(2)}, u32[]{:S(2)}) %collective-permute-start) | collective-permute-done | bytes 131104 | tf_op jit(solution)/shard_map/ppermute | solution.py:446
  10.6 1.2 %collective-permute-done.1.from_left = f32[2,2,64,128]{3,2,1,0:T(8,128)S(1)} collective-permute-done((f32[2,2,64,128]{3,2,1,0:T(8,128)S(1)}, f32[2,2,64,128]{3,2,1,0:T(8,128)S(1)}, u32[]{:S(2)}, u32[]{:S(2)}) %collective-permute-start.1) | collective-permute-done | bytes 131104 | tf_op jit(solution)/shard_map/ppermute | solution.py:446
  11.7 0.1 merge.1.refs_3_
  11.8 0.1 collective-permute-start.3
  11.9 0.0 collective-permute-done.2.refs_4_
  11.9 1.5 %collective-permute-done.3.refs_5_ = f32[4,2,64,128]{3,2,1,0:T(8,128)S(1)} collective-permute-done((f32[4,2,64,128]{3,2,1,0:T(8,128)S(1)}, f32[4,2,64,128]{3,2,1,0:T(8,128)S(1)}, u32[]{:S(2)}, u32[]{:S(2)}) %collective-permute-start.3) | collective-permute-done | bytes 262176 | tf_op jit(solution)/shard_map/ppermute | solution.py:446
  13.4 4.3 %cycles.1 = (f32[1,2,64,128]{3,2,1,0:T(8,128)}, f32[1,2,64,128]{3,2,1,0:T(8,128)}, f32[2,64,128]{2,1,0:T(8,128)S(1)}) custom-call(s32[1,5]{1,0:T(1,128)} %refs_0_.1, f32[1,5]{1,0:T(1,128)} %refs_1_.1, f32[4,2,64,128]{3,2,1,0:T(8,128)S(1)} %get-tuple-element.9.refs_2_, f32[4,2,64,128]{3,2,1,0:T(8,128)S(1)} %merge.1.refs_3_, ...), custom_call_target="tpu_custom_call" | custom-call | tf_op jit(solution)/shard_map/cycles/pallas_call | solution.py:519
  17.8 2.7 %collective-permute-start.6 = (f32[2,64,128]{2,1,0:T(8,128)S(1)}, f32[2,64,128]{2,1,0:T(8,128)S(1)}, u32[]{:S(2)}, u32[]{:S(2)}) collective-permute-start(f32[2,64,128]{2,1,0:T(8,128)S(1)} %get-tuple-element.14), channel_id=1, source_target_pairs={{0,24},{8,16},{16,8},{24,0},{1,25},{9,17},{17,9},{25,1},{2,26},{10... | collective-permute-start | bytes 196616 | tf_op jit(solution)/shard_map/ppermute | solution.py:451
  20.5 0.5 %collective-permute-start.5 = (f32[2,64,128]{2,1,0:T(8,128)S(1)}, f32[2,64,128]{2,1,0:T(8,128)S(1)}, u32[]{:S(2)}, u32[]{:S(2)}) collective-permute-start(f32[2,64,128]{2,1,0:T(8,128)S(1)} %get-tuple-element.14), channel_id=1, source_target_pairs={{0,16},{8,24},{16,0},{24,8},{1,17},{9,25},{17,1},{25,9},{2,18},{10... | collective-permute-start | bytes 196616 | tf_op jit(solution)/shard_map/ppermute | solution.py:451
  21.0 0.3 %collective-permute-start.4 = (f32[2,64,128]{2,1,0:T(8,128)S(1)}, f32[2,64,128]{2,1,0:T(8,128)S(1)}, u32[]{:S(2)}, u32[]{:S(2)}) collective-permute-start(f32[2,64,128]{2,1,0:T(8,128)S(1)} %get-tuple-element.14), channel_id=1, source_target_pairs={{0,8},{8,0},{16,24},{24,16},{1,9},{9,1},{17,25},{25,17},{2,10},{10... | collective-permute-start | bytes 196616 | tf_op jit(solution)/shard_map/ppermute | solution.py:451
  21.3 1.7 %collective-permute-done.6 = f32[2,64,128]{2,1,0:T(8,128)S(1)} collective-permute-done((f32[2,64,128]{2,1,0:T(8,128)S(1)}, f32[2,64,128]{2,1,0:T(8,128)S(1)}, u32[]{:S(2)}, u32[]{:S(2)}) %collective-permute-start.6) | collective-permute-done | bytes 65568 | tf_op jit(solution)/shard_map/ppermute | solution.py:451
  23.0 1.7 %collective-permute-done.5 = f32[2,64,128]{2,1,0:T(8,128)S(1)} collective-permute-done((f32[2,64,128]{2,1,0:T(8,128)S(1)}, f32[2,64,128]{2,1,0:T(8,128)S(1)}, u32[]{:S(2)}, u32[]{:S(2)}) %collective-permute-start.5) | collective-permute-done | bytes 65568 | tf_op jit(solution)/shard_map/ppermute | solution.py:451
  24.8 0.5 %collective-permute-done.4 = f32[2,64,128]{2,1,0:T(8,128)S(1)} collective-permute-done((f32[2,64,128]{2,1,0:T(8,128)S(1)}, f32[2,64,128]{2,1,0:T(8,128)S(1)}, u32[]{:S(2)}, u32[]{:S(2)}) %collective-permute-start.4) | collective-permute-done | bytes 65568 | tf_op jit(solution)/shard_map/ppermute | solution.py:451
  25.3 0.6 %add_add_fusion = f32[2,64,128]{2,1,0:T(8,128)} fusion(f32[2,64,128]{2,1,0:T(8,128)S(1)} %collective-permute-done.5, f32[2,64,128]{2,1,0:T(8,128)S(1)} %collective-permute-done.6, f32[2,64,128]{2,1,0:T(8,128)S(1)} %get-tuple-element.14, f32[2,64,128]{2,1,0:T(8,128)S(1)} %collective-permute-done.4), kind=kLoop, calls=%fused_computation | loop fusion | flops 49152 | bytes 327680 | tf_op jit(solution)/shard_map/add | solution.py:454
Async XLA Ops:
  2.1 8.4 %collective-permute-start = (f32[2,2,64,128]{3,2,1,0:T(8,128)S(1)}, f32[2,2,64,128]{3,2,1,0:T(8,128)S(1)}, u32[]{:S(2)}, u32[]{:S(2)}) collective-permute-start(f32[2,2,64,128]{3,2,1,0:T(8,128)S(1)} %get-tuple-element.10), channel_id=1, source_target_pairs={{1,0},{2,1},{3,2},{5,4},{6,5},{7,6},{9,8},{10,9},{11,10},{13,12},{... | collective-permute-start | bytes 393224 | tf_op jit(solution)/shard_map/ppermute | solution.py:446
  3.4 8.3 %collective-permute-start.1 = (f32[2,2,64,128]{3,2,1,0:T(8,128)S(1)}, f32[2,2,64,128]{3,2,1,0:T(8,128)S(1)}, u32[]{:S(2)}, u32[]{:S(2)}) collective-permute-start(f32[2,2,64,128]{3,2,1,0:T(8,128)S(1)} %get-tuple-element.11), channel_id=1, source_target_pairs={{0,1},{1,2},{2,3},{4,5},{5,6},{6,7},{8,9},{9,10},{10,11},{12,13},{... | collective-permute-start | bytes 393224 | tf_op jit(solution)/shard_map/ppermute | solution.py:446
  9.0 2.9 %collective-permute-start.2 = (f32[4,2,64,128]{3,2,1,0:T(8,128)S(1)}, f32[4,2,64,128]{3,2,1,0:T(8,128)S(1)}, u32[]{:S(2)}, u32[]{:S(2)}) collective-permute-start(f32[4,2,64,128]{3,2,1,0:T(8,128)S(1)} %get-tuple-element.9.refs_2_), channel_id=1, source_target_pairs={{4,0},{0,4},{5,1},{1,5},{6,2},{2,6},{7,3},{3,7},{12,8},{8,12},{13,... | collective-permute-start | bytes 786440 | tf_op jit(solution)/shard_map/ppermute | solution.py:446
  11.8 1.6 %collective-permute-start.3 = (f32[4,2,64,128]{3,2,1,0:T(8,128)S(1)}, f32[4,2,64,128]{3,2,1,0:T(8,128)S(1)}, u32[]{:S(2)}, u32[]{:S(2)}) collective-permute-start(f32[4,2,64,128]{3,2,1,0:T(8,128)S(1)} %merge.1.refs_3_), channel_id=1, source_target_pairs={{4,0},{0,4},{5,1},{1,5},{6,2},{2,6},{7,3},{3,7},{12,8},{8,12},{13,... | collective-permute-start | bytes 786440 | tf_op jit(solution)/shard_map/ppermute | solution.py:446
  17.8 5.2 %collective-permute-start.6 = (f32[2,64,128]{2,1,0:T(8,128)S(1)}, f32[2,64,128]{2,1,0:T(8,128)S(1)}, u32[]{:S(2)}, u32[]{:S(2)}) collective-permute-start(f32[2,64,128]{2,1,0:T(8,128)S(1)} %get-tuple-element.14), channel_id=1, source_target_pairs={{0,24},{8,16},{16,8},{24,0},{1,25},{9,17},{17,9},{25,1},{2,26},{10... | collective-permute-start | bytes 196616 | tf_op jit(solution)/shard_map/ppermute | solution.py:451
  20.5 4.3 %collective-permute-start.5 = (f32[2,64,128]{2,1,0:T(8,128)S(1)}, f32[2,64,128]{2,1,0:T(8,128)S(1)}, u32[]{:S(2)}, u32[]{:S(2)}) collective-permute-start(f32[2,64,128]{2,1,0:T(8,128)S(1)} %get-tuple-element.14), channel_id=1, source_target_pairs={{0,16},{8,24},{16,0},{24,8},{1,17},{9,25},{17,1},{25,9},{2,18},{10... | collective-permute-start | bytes 196616 | tf_op jit(solution)/shard_map/ppermute | solution.py:451
  21.0 4.3 %collective-permute-start.4 = (f32[2,64,128]{2,1,0:T(8,128)S(1)}, f32[2,64,128]{2,1,0:T(8,128)S(1)}, u32[]{:S(2)}, u32[]{:S(2)}) collective-permute-start(f32[2,64,128]{2,1,0:T(8,128)S(1)} %get-tuple-element.14), channel_id=1, source_target_pairs={{0,8},{8,0},{16,24},{24,16},{1,9},{9,1},{17,25},{25,17},{2,10},{10... | collective-permute-start | bytes 196616 | tf_op jit(solution)/shard_map/ppermute | solution.py:451
